TPU v7x, 256 devices: a whole 4x4x8 slice. The times are simulated.
256 devices in a mesh: batch: 8 (over x, core), branch: 32 (over z, y).
Axes of the slice: x: 4, y: 4, z: 8, core: 2. Of those that a mesh axis runs over, the one named last changes fastest.
Arguments:
- queries: bfloat16 [256, 128, 16, 128], P(('batch', 'branch')), parts along dimension 0, may hold values from -6 to 6
- response_keys: bfloat16 [256, 128, 4, 128], P(('batch', 'branch')), parts along dimension 0, may hold values from -6 to 6
- response_values: bfloat16 [256, 128, 4, 128], P(('batch', 'branch')), parts along dimension 0, may hold values from -6 to 6
- prompt_keys: bfloat16 [16384, 4, 128], P(('batch', 'branch')), parts along dimension 0, may hold values from -6 to 6
- prompt_value_rows: bfloat16 [16384, 4, 128], P(('batch', 'branch')), parts along dimension 0, may hold values from -6 to 6
- lengths: int32 [256], P(('batch', 'branch')), parts along dimension 0, may hold values from 16 to 128, as said below
- grad_out: bfloat16 [256, 128, 16, 128], P(('batch', 'branch')), parts along dimension 0, may hold values from -6 to 6
Outputs:
- attended: bfloat16 [256, 128, 16, 128], P(('batch', 'branch')), parts along dimension 0
- grad_query: bfloat16 [256, 128, 16, 128], P(('batch', 'branch')), parts along dimension 0
- grad_resp_keys: bfloat16 [256, 128, 4, 128], P(('batch', 'branch')), parts along dimension 0
- grad_resp_values: bfloat16 [256, 128, 4, 128], P(('batch', 'branch')), parts along dimension 0
- grad_prompt_keys: bfloat16 [16384, 4, 128], P(('batch', 'branch')), parts along dimension 0
- grad_prompt_values: bfloat16 [16384, 4, 128], P(('batch', 'branch')), parts along dimension 0
There are 8 independent parts, one for each index of `batch`. A program takes and returns all parts, laid end to end along the dimension named above; each array names one. Nothing has to cross between parts.
Inputs may be any that keep to these rules, and one draw needn't show every extreme that they name: `lengths`: some response of every prompt has all 128 slots live.
All inputs are finite; a program needn't handle non-finite values.
Results may differ from a plain program's by a relative error of at most 0.034.
Values may be sent and summed in bfloat16 or wider, within the bound.
No kernel may reach another device: no remote copies, remote signals or barrier semaphores. Data moves between devices by JAX's collectives and lax.ppermute only.
A program may use at most 192 MiB of HBM per device.

v0:
```python
import jax
import jax.numpy as jnp
from jax import lax
from jax.sharding import PartitionSpec as P

masked_score = -1e30


def local_attention(
    queries, response_keys, response_values, whole_keys, whole_values, lengths, grad_out
):
    resp_count, seq_len, num_heads, head_dim = queries.shape
    kv_heads = whole_keys.shape[1]
    group_size = num_heads // kv_heads
    score_scale = head_dim ** (-0.5)
    grouped = queries.reshape(resp_count, seq_len, kv_heads, group_size, head_dim)
    row_ids = jnp.arange(seq_len)
    causal = row_ids[None, :] <= row_ids[:, None]
    live_rows = row_ids[None, :] < lengths[:, None]
    live_wide = live_rows[:, :, None, None, None]
    grad_grouped = grad_out.reshape(resp_count, seq_len, kv_heads, group_size, head_dim)
    masked = jnp.where(live_wide, grad_grouped, jnp.zeros_like(grad_grouped))
    prompt_scores = (
        jnp.einsum("rtkgd,skd->rkgts", grouped, whole_keys, preferred_element_type=jnp.float32)
        * score_scale
    )
    own_scores = (
        jnp.einsum("rtkgd,rskd->rkgts", grouped, response_keys, preferred_element_type=jnp.float32)
        * score_scale
    )
    own_scores = jnp.where(causal, own_scores, masked_score)
    top_score = jnp.maximum(
        jnp.max(prompt_scores, axis=-1, keepdims=True), jnp.max(own_scores, axis=-1, keepdims=True)
    )
    total = jnp.sum(jnp.exp(prompt_scores - top_score), axis=-1, keepdims=True) + jnp.sum(
        jnp.exp(own_scores - top_score), axis=-1, keepdims=True
    )
    log_total = top_score + jnp.log(total)
    prompt_weights = jnp.exp(prompt_scores - log_total)
    own_weights = jnp.exp(own_scores - log_total)
    prompt_low = prompt_weights.astype(jnp.bfloat16)
    own_low = own_weights.astype(jnp.bfloat16)
    attended = jnp.einsum(
        "rkgts,skd->rtkgd", prompt_low, whole_values, preferred_element_type=jnp.float32
    )
    attended = attended + jnp.einsum(
        "rkgts,rskd->rtkgd", own_low, response_values, preferred_element_type=jnp.float32
    )
    attended = jnp.where(live_wide, attended, 0.0).astype(jnp.bfloat16)
    row_delta = jnp.sum(masked.astype(jnp.float32) * attended.astype(jnp.float32), axis=-1)
    row_delta = jnp.transpose(row_delta, (0, 2, 3, 1))
    prompt_dw = jnp.einsum(
        "rtkgd,skd->rkgts", masked, whole_values, preferred_element_type=jnp.float32
    )
    own_dw = jnp.einsum(
        "rtkgd,rskd->rkgts", masked, response_values, preferred_element_type=jnp.float32
    )
    prompt_ds = (prompt_weights * (prompt_dw - row_delta[..., None])).astype(jnp.bfloat16)
    own_ds = (own_weights * (own_dw - row_delta[..., None])).astype(jnp.bfloat16)
    grad_query = jnp.einsum(
        "rkgts,skd->rtkgd", prompt_ds, whole_keys, preferred_element_type=jnp.float32
    )
    grad_query = grad_query + jnp.einsum(
        "rkgts,rskd->rtkgd", own_ds, response_keys, preferred_element_type=jnp.float32
    )
    grad_query = (grad_query * score_scale).astype(jnp.bfloat16)
    grad_rk = (
        jnp.einsum("rkgts,rtkgd->rskd", own_ds, grouped, preferred_element_type=jnp.float32)
        * score_scale
    ).astype(jnp.bfloat16)
    grad_rv = jnp.einsum(
        "rkgts,rtkgd->rskd", own_low, masked, preferred_element_type=jnp.float32
    ).astype(jnp.bfloat16)
    return (
        attended.reshape(resp_count, seq_len, num_heads, head_dim),
        grad_query.reshape(resp_count, seq_len, num_heads, head_dim),
        grad_rk,
        grad_rv,
        prompt_ds,
        prompt_low,
        grouped,
        masked,
        log_total[..., 0],
        row_delta,
    )


def take_rows(prompt_dk, prompt_dv):
    return jnp.stack([prompt_dk, prompt_dv], axis=1)


def on_device(
    queries, response_keys, response_values, prompt_keys, prompt_value_rows, lengths, grad_out
):
    whole_keys, whole_values = (
        lax.all_gather(prompt_keys, "branch", axis=0, tiled=True),
        lax.all_gather(prompt_value_rows, "branch", axis=0, tiled=True),
    )
    (
        attended,
        grad_query,
        grad_rk,
        grad_rv,
        prompt_ds,
        prompt_low,
        grouped,
        masked,
        log_total,
        row_delta,
    ) = local_attention(
        queries, response_keys, response_values, whole_keys, whole_values, lengths, grad_out
    )
    score_scale = queries.shape[-1] ** (-0.5)
    local_dk = (
        jnp.einsum("rkgts,rtkgd->skd", prompt_ds, grouped, preferred_element_type=jnp.float32)
        * score_scale
    )
    local_dv = jnp.einsum(
        "rkgts,rtkgd->skd", prompt_low, masked, preferred_element_type=jnp.float32
    )
    shares = lax.psum_scatter(
        take_rows(local_dk, local_dv).astype(jnp.bfloat16),
        "branch",
        scatter_dimension=0,
        tiled=True,
    ).astype(jnp.float32)
    prompt_dk = shares[:, 0]
    prompt_dv = shares[:, 1]
    return (
        attended,
        grad_query,
        grad_rk,
        grad_rv,
        prompt_dk.astype(jnp.bfloat16),
        prompt_dv.astype(jnp.bfloat16),
    )


def solution(mesh):
    return jax.shard_map(
        on_device,
        mesh=mesh,
        in_specs=(
            P(("batch", "branch"), None, None, None),
            P(("batch", "branch"), None, None, None),
            P(("batch", "branch"), None, None, None),
            P(("batch", "branch"), None, None),
            P(("batch", "branch"), None, None),
            P(("batch", "branch")),
            P(("batch", "branch"), None, None, None),
        ),
        out_specs=(
            P(("batch", "branch"), None, None, None),
            P(("batch", "branch"), None, None, None),
            P(("batch", "branch"), None, None, None),
            P(("batch", "branch"), None, None, None),
            P(("batch", "branch"), None, None),
            P(("batch", "branch"), None, None),
        ),
        check_vma=False,
    )
```

profile of v0, /device:TPU:2, one launch (start us, length us, event | category | flops | bytes accessed | tf_op | source)
XLA Modules:
  0.0 424.4 jit_solution(5410509129297976514)
XLA Ops:
  7.2 1.5 copy.13
  8.8 0.0 all-gather.5.cloned.1.call-start
  8.8 1.5 copy.17
  10.3 0.0 reduce-scatter.2.cloned.1.call-start
  10.4 2.2 copy.24
  13.3 1.5 copy.21
  14.8 1.2 fusion.65
  16.0 76.1 %all-gather.3.cloned.1.call-done = bf16[2048,4,128]{2,0,1:T(8,128)(2,1)} async-done(((bf16[64,4,128]{2,0,1:T(8,128)(2,1)}), bf16[2048,4,128]{2,0,1:T(8,128)(2,1)}) %all-gather.3.cloned.1.call-update) | async-done | bytes 2097168 | tf_op jit(solution)/shard_map/all_gather | solution.py:96
  92.2 9.7 %bitcast_reduce_fusion = (f32[4,4,128]{2,1,0:T(4,128)S(1)}, f32[4,2048,128,4]{2,1,3,0:T(8,128)}) fusion(bf16[128,4,4,128]{3,2,1,0:T(4,128)(2,1)S(1)} %bitcast.201, bf16[2048,4,128]{2,0,1:T(8,128)(2,1)} %all-gather.3.cloned.1.call-done), kind=kOutput, calls=%fused_computation.5 | convolution fusion | flops 1082128384 | bytes 19406848 | tf_op jit(solution)/shard_map/rtkgd,skd->rkgts/dot_general | solution.py:24
  101.8 0.2 exponential_reduce_fusion
  102.0 8.6 %fusion.3 = f32[4,4,128]{2,1,0:T(4,128)S(1)} fusion(f32[4,2048,128,4]{2,1,3,0:T(8,128)} %get-tuple-element.15, f32[4,4,128]{2,1,0:T(4,128)S(1)} %max.11), kind=kLoop, calls=%fused_computation.7 | loop fusion | flops 12580864 | bytes 16793600 | tf_op jit(solution)/shard_map/reduce_sum | solution.py:35
  110.6 10.0 %fusion.9 = bf16[2048,1,4,128]{3,0,2,1:T(8,128)(2,1)} fusion(f32[4,2048,128,4]{2,1,3,0:T(8,128)} %get-tuple-element.15, f32[4,4,128]{2,1,0:T(4,128)S(1)} %bitcast.213, bf16[128,4,4,128]{0,3,2,1:T(8,128)(2,1)S(1)} %copy.21, pred[128]{0:T(512)(128)(4,1)S(1)} %iota_compare_fusion.1), kind=kOutput, calls=%fused_computation.16 | convolution fusion | flops 1087635456 | bytes 19406976 | tf_op jit(solution)/shard_map/rkgts,rtkgd->skd/dot_general | solution.py:118
  120.6 49.9 %all-gather.5.cloned.1.call-done = bf16[2048,4,128]{2,0,1:T(8,128)(2,1)} async-done(((bf16[64,4,128]{2,0,1:T(8,128)(2,1)}), bf16[2048,4,128]{2,0,1:T(8,128)(2,1)}) %all-gather.5.cloned.1.call-update) | async-done | bytes 2097168 | tf_op jit(solution)/shard_map/all_gather | solution.py:97
  170.5 8.1 %fusion.18 = f32[1,128,4,4,128]{1,4,3,2,0:T(8,128)S(1)} fusion(bf16[2048,4,128]{2,0,1:T(8,128)(2,1)} %all-gather.5.cloned.1.call-done, f32[4,2048,128,4]{2,1,3,0:T(8,128)} %get-tuple-element.15, f32[4,4,128]{2,1,0:T(4,128)S(1)} %bitcast.214), kind=kOutput, calls=%fused_computation.25 | convolution fusion | flops 1086324736 | bytes 19931136 | tf_op jit(solution)/shard_map/rkgts,skd->rtkgd/dot_general | solution.py:43
  178.6 2.3 multiply_reduce_fusion
  180.9 8.5 %fusion.7 = bf16[4,4,128,2048]{2,3,1,0:T(8,128)(2,1)S(1)} fusion(f32[4,2048,128,4]{2,1,3,0:T(8,128)} %get-tuple-element.15, f32[4,4,128]{2,1,0:T(4,128)S(1)} %bitcast.220, f32[4,4,128]{2,1,0:T(4,128)S(1)} %bitcast.216, bf16[2048,4,128]{2,0,1:T(8,128)(2,1)} %all-gather.5.cloned.1.call-done, bf16[128,4,4,128]{0,3,2,1:T(8,128)(2,1)S(1)} %copy.21, ...), kind=kOutput, calls=%fused_computation.11 | convolution fusion | flops 1094975488 | bytes 27803776 | tf_op jit(solution)/shard_map/rtkgd,skd->rkgts/dot_general | solution.py:52
  189.4 3.2 copy-done.1
  192.6 2.4 fusion.10
  195.0 2.3 pad_maximum_fusion
  197.3 1.2 copy.36
  198.5 0.3 fusion.35
  198.9 6.9 %fusion.21 = f32[1,128,4,4,128]{4,1,3,2,0:T(8,128)S(1)} fusion(bf16[4,4,128,2048]{2,3,1,0:T(8,128)(2,1)} %copy-done.1, bf16[2048,4,128]{2,0,1:T(8,128)(2,1)} %all-gather.3.cloned.1.call-done), kind=kOutput, calls=%fused_computation.26 | convolution fusion | flops 1073741824 | bytes 11534336 | tf_op jit(solution)/shard_map/rkgts,skd->rtkgd/dot_general | solution.py:60
  205.8 0.4 fusion.33
  206.2 1.1 copy.37
  207.3 0.3 fusion.42
  207.6 0.8 copy.38
  208.3 0.3 fusion.41
  208.7 0.8 copy.39
  209.5 206.2 %reduce-scatter.2.cloned.1.call-done = bf16[64,2,4,128]{3,0,2,1:T(8,128)(2,1)} async-done(((bf16[2048,2,4,128]{3,0,2,1:T(8,128)(2,1)}), bf16[64,2,4,128]{3,0,2,1:T(8,128)(2,1)}) %reduce-scatter.2.cloned.1.call-update) | async-done | bytes 131088 | tf_op jit(solution)/shard_map/reduce_scatter | solution.py:121
  415.7 0.9 slice_bitcast_fusion
  416.5 0.7 copy.40
  417.2 0.7 copy.41
  (19 shorter events, 0.2 us)
Async XLA Ops:
  7.2 7.6 %copy-start = (bf16[1,128,16,128]{3,2,1,0:T(8,128)(2,1)S(1)}, bf16[1,128,16,128]{3,2,1,0:T(8,128)(2,1)}, u32[]{:S(2)}) copy-start(bf16[1,128,16,128]{3,2,1,0:T(8,128)(2,1)} %param.7) | copy-start | bytes 1572868
  7.2 85.0 %all-gather.3.cloned.1.call-start = ((), (), s32[]{:S(2)}) async-start(), calls=%async_computation.1 | async-start | bytes 2162688 | tf_op jit(solution)/shard_map/all_gather | solution.py:96
  8.8 161.7 %all-gather.5.cloned.1.call-start = ((), (), s32[]{:S(2)}) async-start(), calls=%async_computation.2 | async-start | bytes 2162688 | tf_op jit(solution)/shard_map/all_gather | solution.py:97
  10.3 405.3 %reduce-scatter.2.cloned.1.call-start = ((), (), s32[]{:S(2)}) async-start(), calls=%async_computation.3 | async-start | bytes 4325376 | tf_op jit(solution)/shard_map/reduce_scatter | solution.py:121
  120.6 58.0 %copy-start.4 = (bf16[1,128,4,128]{3,2,1,0:T(4,128)(2,1)S(1)}, bf16[1,128,4,128]{3,2,1,0:T(4,128)(2,1)}, u32[]{:S(2)}) copy-start(bf16[1,128,4,128]{3,2,1,0:T(4,128)(2,1)} %param.9) | copy-start | bytes 393220
  189.4 3.2 copy-start.1
  192.6 2.4 copy-start.2
  195.0 2.4 copy-start.3
  198.8 6.9 %copy-start.5 = (bf16[1,128,4,128]{3,2,1,0:T(4,128)(2,1)S(1)}, bf16[1,128,4,128]{3,2,1,0:T(4,128)(2,1)}, u32[]{:S(2)}) copy-start(bf16[1,128,4,128]{3,2,1,0:T(4,128)(2,1)} %param.8) | copy-start | bytes 393220
Sparse Core Ops, SparseCore 0:
  11.2 80.9 all-gather.2
  95.3 75.0 all-gather.4
  197.4 218.1 reduce-scatter.1
where the time goes:
time: 425 us; the launch traced here: 424 us
  waiting for transfers between devices  332 us (78%)
  matrix products  50.3 us (12%)
  local copies, waits for them, and re-layouts  16.1 us (4%)
  between operations  14.6 us (3%)
  other arithmetic  11.1 us (3%)
    reduce_scatter x1, waiting for transfers between devices, on_device(): lax.psum_scatter(take_rows(local_dk, local_dv).astype(jnp.bfloat16), 'bra...  206 us
    all_gather x1, waiting for transfers between devices, on_device(): lax.all_gather(prompt_keys, 'branch', axis=0, tiled=True)  76.1 us
    all_gather x1, waiting for transfers between devices, on_device(): lax.all_gather(prompt_value_rows, 'branch', axis=0, tiled=True)  49.9 us
    unnamed x21, local copies, waits for them, and re-layouts  13.7 us
    dot_general x1, matrix products, on_device(): jnp.einsum('rkgts,rtkgd->skd', prompt_low, masked, preferred_element_type...  9.96 us
    dot_general x1, matrix products, local_attention(): jnp.einsum('rtkgd,skd->rkgts', grouped, whole_keys, preferred_element_typ...  9.66 us
    reduce_sum x1, other arithmetic, local_attention(): jnp.sum(jnp.exp(prompt_scores - top_score), axis=-1, keepdims=True)  8.57 us
  transfers between devices with their start and end apart: 3, of which 3 were waited for; matrix products, arithmetic and copies ran while one was open for 11% of the time, Pallas kernels for 0%

commit v1 on v0

--- a/solution.py
+++ b/solution.py
@@ -4,6 +4,11 @@
 from jax.sharding import PartitionSpec as P
 
 masked_score = -1e30
+
+
+def swapped_in(x, axis, along):
+    stack = jnp.stack([x] * lax.axis_size(axis))
+    return jnp.concatenate(lax.all_to_all(stack, axis, 0, 0), axis=along)
 
 
 def local_attention(
@@ -94,7 +99,7 @@
 ):
     whole_keys, whole_values = (
         lax.all_gather(prompt_keys, "branch", axis=0, tiled=True),
-        lax.all_gather(prompt_value_rows, "branch", axis=0, tiled=True),
+        swapped_in(prompt_value_rows, "branch", 0),
     )
     (
         attended,

time: 425 us -> 383 us (0.901)
  waiting for transfers between devices: 332 us -> 277 us
  starting transfers between devices: 0.12 us -> 11.7 us
    all_gather x1 -> x0, waiting for transfers between devices: 49.9 us -> none  [on_device(): lax.all_gather(prompt_value_rows, 'branch', axis=0, tiled=True)]
    all_to_all x0 -> x1, starting transfers between devices: none -> 11.6 us  [swapped_in(): return jnp.concatenate(lax.all_to_all(stack, axis, 0, 0), axis=along)]
    all_gather x1, waiting for transfers between devices: 76.1 us -> 70.8 us  [on_device(): lax.all_gather(prompt_keys, 'branch', axis=0, tiled=True)]
    unnamed x21 -> x29, local copies, waits for them, and re-layouts: 13.7 us -> 13.1 us
  transfers between devices with their start and end apart: 3 -> 3, of which waited for: 3 -> 2; matrix products, arithmetic and copies ran while one was open for 11% -> 10% of each run, Pallas kernels for 0% -> 0%
where the time goes in v1:
time: 383 us; the launch traced here: 382 us
  waiting for transfers between devices  277 us (72%)
  matrix products  48.5 us (13%)
  local copies, waits for them, and re-layouts  19.1 us (5%)
  between operations  14.9 us (4%)
  starting transfers between devices  11.7 us (3%)
  other arithmetic  11.1 us (3%)
    reduce_scatter x1, waiting for transfers between devices, on_device(): lax.psum_scatter(take_rows(local_dk, local_dv).astype(jnp.bfloat16), 'bra...  206 us
    all_gather x1, waiting for transfers between devices, on_device(): lax.all_gather(prompt_keys, 'branch', axis=0, tiled=True)  70.8 us
    unnamed x29, local copies, waits for them, and re-layouts  13.1 us
    all_to_all x1, starting transfers between devices, swapped_in(): return jnp.concatenate(lax.all_to_all(stack, axis, 0, 0), axis=along)  11.6 us
    dot_general x1, matrix products, local_attention(): jnp.einsum('rkgts,skd->rtkgd', prompt_low, whole_values, preferred_elemen...  9.77 us
    dot_general x1, matrix products, local_attention(): jnp.einsum('rtkgd,skd->rkgts', grouped, whole_keys, preferred_element_typ...  9.67 us
    dot_general x1, matrix products, on_device(): jnp.einsum('rkgts,rtkgd->skd', prompt_low, masked, preferred_element_type...  9 us
    reduce_sum x1, other arithmetic, local_attention(): jnp.sum(jnp.exp(prompt_scores - top_score), axis=-1, keepdims=True)  8.54 us
  transfers between devices with their start and end apart: 3, of which 2 were waited for; matrix products, arithmetic and copies ran while one was open for 10% of the time, Pallas kernels for 0%

profile of v1, /device:TPU:2, one launch (start us, length us, event | category | flops | bytes accessed | tf_op | source)
XLA Modules:
  0.0 382.4 jit_solution(14626327553298380470)
XLA Ops:
  7.2 1.5 copy.73
  8.8 0.9 copy.77
  9.7 1.8 stack.11
  11.5 11.6 %all-to-all-start = ((bf16[32,64,4,128]{3,1,2,0:T(8,128)(2,1)}), bf16[32,64,4,128]{3,1,2,0:T(8,128)(2,1)}, u32[]{:S(2)}, u32[]{:S(2)}) async-start(bf16[32,64,4,128]{3,1,2,0:T(8,128)(2,1)} %stack.11), calls=%async_computation | async-start | bytes 4194304 | tf_op jit(solution)/shard_map/all_to_all | solution.py:11
  23.2 2.2 copy.86
  26.1 1.5 copy.83
  27.6 0.3 fusion.59
  27.9 70.8 %all-gather.2.cloned.1.call-done = bf16[2048,4,128]{2,0,1:T(8,128)(2,1)} async-done(((bf16[64,4,128]{2,0,1:T(8,128)(2,1)}), bf16[2048,4,128]{2,0,1:T(8,128)(2,1)}) %all-gather.2.cloned.1.call-update) | async-done | bytes 2097168 | tf_op jit(solution)/shard_map/all_gather | solution.py:101
  98.7 9.7 %bitcast_reduce_fusion = (f32[4,4,128]{2,1,0:T(4,128)S(1)}, f32[4,2048,128,4]{2,1,3,0:T(8,128)}) fusion(bf16[128,4,4,128]{3,2,1,0:T(4,128)(2,1)S(1)} %bitcast.202, bf16[2048,4,128]{2,0,1:T(8,128)(2,1)} %all-gather.2.cloned.1.call-done), kind=kOutput, calls=%fused_computation.5 | convolution fusion | flops 1082128384 | bytes 19406848 | tf_op jit(solution)/shard_map/rtkgd,skd->rkgts/dot_general | solution.py:29
  108.4 0.2 exponential_reduce_fusion
  108.6 8.5 %fusion.3 = f32[4,4,128]{2,1,0:T(4,128)S(1)} fusion(f32[4,2048,128,4]{2,1,3,0:T(8,128)} %get-tuple-element.27, f32[4,4,128]{2,1,0:T(4,128)S(1)} %max.11), kind=kLoop, calls=%fused_computation.7 | loop fusion | flops 12580864 | bytes 16793600 | tf_op jit(solution)/shard_map/reduce_sum | solution.py:40
  117.2 1.8 copy.78
  118.9 9.8 %convolution_bitcast_fusion.3 = f32[1,128,4,4,128]{1,4,3,2,0:T(8,128)} fusion(bf16[2048,4,128,1]{2,0,3,1:T(8,128)(2,1)S(1)} %bitcast.206, f32[4,2048,128,4]{2,1,3,0:T(8,128)} %get-tuple-element.27, f32[4,4,128]{2,1,0:T(4,128)S(1)} %bitcast.216), kind=kOutput, calls=%fused_computation.26 | convolution fusion | flops 1086324736 | bytes 19931136 | tf_op jit(solution)/shard_map/rkgts,skd->rtkgd/dot_general | solution.py:48
  128.7 9.0 %fusion.9 = bf16[2048,1,4,128]{3,0,2,1:T(8,128)(2,1)S(1)} fusion(f32[4,2048,128,4]{2,1,3,0:T(8,128)} %get-tuple-element.27, f32[4,4,128]{2,1,0:T(4,128)S(1)} %bitcast.217, bf16[128,4,4,128]{0,3,2,1:T(8,128)(2,1)S(1)} %copy.83, pred[128]{0:T(512)(128)(4,1)S(1)} %iota_compare_fusion.1), kind=kOutput, calls=%fused_computation.16 | convolution fusion | flops 1087635456 | bytes 19406976 | tf_op jit(solution)/shard_map/rkgts,rtkgd->skd/dot_general | solution.py:123
  137.8 1.2 multiply_reduce_fusion
  139.0 7.9 %fusion.7 = bf16[4,4,128,2048]{2,3,1,0:T(8,128)(2,1)S(1)} fusion(f32[4,2048,128,4]{2,1,3,0:T(8,128)} %get-tuple-element.27, f32[4,4,128]{2,1,0:T(4,128)S(1)} %bitcast.223, f32[4,4,128]{2,1,0:T(4,128)S(1)} %bitcast.219, bf16[2048,4,128,1]{2,0,3,1:T(8,128)(2,1)S(1)} %bitcast.207, bf16[128,4,4,128]{0,3,2,1:T(8,128)(2,1)S(1)} %copy.83, ...), kind=kOutput, calls=%fused_computation.11 | convolution fusion | flops 1094975488 | bytes 27803776 | tf_op jit(solution)/shard_map/rtkgd,skd->rkgts/dot_general | solution.py:57
  146.9 3.2 copy-done.1
  150.1 2.3 fusion.10
  152.5 2.3 pad_maximum_fusion
  154.9 1.2 copy.98
  156.1 0.3 fusion.29
  156.4 6.9 %fusion.15 = f32[1,128,4,4,128]{4,1,3,2,0:T(8,128)S(1)} fusion(bf16[4,4,128,2048]{2,3,1,0:T(8,128)(2,1)} %copy-done.1, bf16[2048,4,128]{2,0,1:T(8,128)(2,1)} %all-gather.2.cloned.1.call-done), kind=kOutput, calls=%fused_computation.22 | convolution fusion | flops 1073741824 | bytes 11534336 | tf_op jit(solution)/shard_map/rkgts,skd->rtkgd/dot_general | solution.py:65
  163.3 0.4 fusion.27
  163.7 1.1 copy.99
  164.8 0.3 fusion.36
  165.1 0.8 copy.100
  165.9 0.3 fusion.35
  166.2 0.8 copy.101
  167.0 206.4 %reduce-scatter.2.cloned.1.call-done = bf16[64,2,4,128]{3,0,2,1:T(8,128)(2,1)} async-done(((bf16[2048,2,4,128]{3,0,2,1:T(8,128)(2,1)}), bf16[64,2,4,128]{3,0,2,1:T(8,128)(2,1)}) %reduce-scatter.2.cloned.1.call-update) | async-done | bytes 131088 | tf_op jit(solution)/shard_map/reduce_scatter | solution.py:126
  373.4 0.9 slice_bitcast_fusion
  374.2 0.7 copy.102
  374.9 0.7 copy.103
  (28 shorter events, 0.2 us)
Async XLA Ops:
  7.2 20.4 %copy-start = (bf16[1,128,16,128]{3,2,1,0:T(8,128)(2,1)S(1)}, bf16[1,128,16,128]{3,2,1,0:T(8,128)(2,1)}, u32[]{:S(2)}) copy-start(bf16[1,128,16,128]{3,2,1,0:T(8,128)(2,1)} %param.7) | copy-start | bytes 1572868
  7.2 20.4 %copy-start.9 = (bf16[1,128,4,128]{3,2,1,0:T(4,128)(2,1)S(1)}, bf16[1,128,4,128]{3,2,1,0:T(4,128)(2,1)}, u32[]{:S(2)}) copy-start(bf16[1,128,4,128]{3,2,1,0:T(4,128)(2,1)} %param.8) | copy-start | bytes 393220
  7.2 91.6 %all-gather.2.cloned.1.call-start = ((), (), s32[]{:S(2)}) async-start(), calls=%async_computation.2 | async-start | bytes 2162688 | tf_op jit(solution)/shard_map/all_gather | solution.py:101
  11.5 105.7 %all-to-all-start = ((bf16[32,64,4,128]{3,1,2,0:T(8,128)(2,1)}), bf16[32,64,4,128]{3,1,2,0:T(8,128)(2,1)}, u32[]{:S(2)}, u32[]{:S(2)}) async-start(bf16[32,64,4,128]{3,1,2,0:T(8,128)(2,1)} %stack.11), calls=%async_computation | async-start | bytes 4194304 | tf_op jit(solution)/shard_map/all_to_all | solution.py:11
  23.1 350.2 %reduce-scatter.2.cloned.1.call-start = ((), (), s32[]{:S(2)}) async-start(), calls=%async_computation.3 | async-start | bytes 4325376 | tf_op jit(solution)/shard_map/reduce_scatter | solution.py:126
  27.9 80.5 %copy-start.2 = (f32[1,4,4,128,128]{3,4,2,1,0:T(8,128)}, f32[1,4,4,128,128]{3,4,2,1,0:T(8,128)S(1)}, u32[]{:S(2)}) copy-start(f32[1,4,4,128,128]{3,4,2,1,0:T(8,128)S(1)} %get-tuple-element.29) | copy-start | bytes 3145732
  128.7 9.0 %copy-start.3 = (f32[1,4,4,128,128]{3,4,2,1,0:T(8,128)S(1)}, f32[1,4,4,128,128]{3,4,2,1,0:T(8,128)}, u32[]{:S(2)}) copy-start(f32[1,4,4,128,128]{3,4,2,1,0:T(8,128)} %copy-done.2) | copy-start | bytes 3145732
  128.7 9.0 %copy-start.5 = (f32[1,128,4,4,128]{1,4,3,2,0:T(8,128)S(1)}, f32[1,128,4,4,128]{1,4,3,2,0:T(8,128)}, u32[]{:S(2)}) copy-start(f32[1,128,4,4,128]{1,4,3,2,0:T(8,128)} %convolution_bitcast_fusion.3) | copy-start | bytes 3145732
  128.7 9.0 %copy-start.6 = (bf16[1,128,16,128]{1,3,2,0:T(8,128)(2,1)S(1)}, bf16[1,128,16,128]{1,3,2,0:T(8,128)(2,1)}, u32[]{:S(2)}) copy-start(bf16[1,128,16,128]{1,3,2,0:T(8,128)(2,1)} %copy.86) | copy-start | bytes 1572868
  128.7 9.0 %copy-start.8 = (bf16[1,128,4,128]{3,2,1,0:T(4,128)(2,1)S(1)}, bf16[1,128,4,128]{3,2,1,0:T(4,128)(2,1)}, u32[]{:S(2)}) copy-start(bf16[1,128,4,128]{3,2,1,0:T(4,128)(2,1)} %param.9) | copy-start | bytes 393220
  146.9 3.2 copy-start.1
  152.5 2.4 copy-start.7
  152.5 3.6 copy-start.4
Sparse Core Ops, SparseCore 0:
  11.2 87.5 all-gather.1
  155.0 218.3 reduce-scatter.1
